TPU v7x, 32 devices: a whole 2x2x4 slice. The times are simulated.
32 devices in a mesh: gx: 4 (over y, x), gy: 4 (over z), gz: 2 (over core).
Axes of the slice: x: 2, y: 2, z: 4, core: 2. Of those that a mesh axis runs over, the one named last changes fastest.
Arguments:
- labels: int32 [128, 128, 1024], P('gx', 'gy', 'gz'), may hold values from 0 to 2
- conduct_scale: float32 [128, 128, 1024], P('gx', 'gy', 'gz'), may hold values from 0.3 to 3
- phase_sigma: float32 [3], replicated, may hold values from 0.2 to 5
- source: float32 [128, 128, 1024], P('gx', 'gy', 'gz'), may hold values from -6 to 6
- potential_in: float32 [128, 128, 1024], P('gx', 'gy', 'gz'), may hold values from -6 to 6
- site_voxel: int32 [32768], P(('gx', 'gy', 'gz')), may hold values from 0 to 524287
- site_owner: int32 [32768], P(('gx', 'gy', 'gz')), may hold values from 0 to 31, as said below
- site_pore: int32 [32768], P(('gx', 'gy', 'gz')), may hold values from 0 to 511
- site_live: int32 [32768], P(('gx', 'gy', 'gz')), may hold values 0 or 1
- site_rate: float32 [32768], P(('gx', 'gy', 'gz')), may hold values from 0.05 to 0.5
- tile_press_in: float32 [2, 32768], P(None, ('gx', 'gy', 'gz')), may hold values from 0.05 to 1
- throat_nbr: int32 [8, 16384], P(None, ('gx', 'gy', 'gz')), may hold values from 0 to 16383, as said below
- throat_count: int32 [16384], P(('gx', 'gy', 'gz')), may hold values from 1 to 8
- throat_weight: float32 [8, 16384], P(None, ('gx', 'gy', 'gz')), may hold values from 0.2 to 5
- pore_exchange: float32 [16384], P(('gx', 'gy', 'gz')), may hold values from 0.1 to 1
- pore_press_in: float32 [2, 16384], P(None, ('gx', 'gy', 'gz')), may hold values from 0.1 to 1
Outputs:
- potential: float32 [128, 128, 1024], P('gx', 'gy', 'gz')
- pore_press: float32 [2, 16384], P(None, ('gx', 'gy', 'gz'))
- tile_press: float32 [2, 32768], P(None, ('gx', 'gy', 'gz'))
Inputs may be any that keep to these rules, and one draw needn't show every extreme that they name: `throat_nbr`: pore p belongs to device p // 512; each throat slot names a pore of that same device or of a device whose brick shares a face with its brick. `site_owner`: each site's owner is the device holding the site or a device whose brick shares a face with that device's brick. In the rows of one device no device other than that device is named by more than 64 rows, and some other device by exactly 64.
All inputs are finite; a program needn't handle non-finite values. No bound on the sum of `site_live` on one device may be relied on, other than what follows from the above.
Results may differ from a plain program's by a relative error of at most 0.0003.
Values sent between devices are 32-bit elements; how exact they have to be, the bound alone decides.
A program may use at most 320 MiB of HBM per device.

v0:
```python
import jax
import jax.numpy as jnp
from jax import lax
from jax.sharding import PartitionSpec as P

SWEEPS_E = 4
SWEEPS_G = 2


REACT = 0.1
DK_A = 2.0
DK_B = 0.7
DIFF_M = 1.0
BATH_A = 1.0
BATH_B = 0.2
CURRENT_SCALE = 0.25


def extended(array, sides, width):
    for axis, dim in sides:
        size, length = (lax.axis_size(axis), array.shape[dim])
        up = [(i, (i + 1) % size) for i in range(size - 1)]
        down = [(j, i) for i, j in up]
        last = lax.slice_in_dim(array, length - width, length, axis=dim)
        leading = lax.slice_in_dim(array, 0, width, axis=dim)
        before = lax.ppermute(last, axis, up)
        after = lax.ppermute(leading, axis, down)
        array = jnp.concatenate([before, array, after], axis=dim)
    return array


def conductivity(labels, conduct_scale, phase_sigma):
    table = jnp.where(
        labels == 0, phase_sigma[0], jnp.where(labels == 1, phase_sigma[1], phase_sigma[2])
    )
    return conduct_scale * table


def beside(arr):
    return (
        arr[2:, 1:-1, 1:-1],
        arr[:-2, 1:-1, 1:-1],
        arr[1:-1, 2:, 1:-1],
        arr[1:-1, :-2, 1:-1],
        arr[1:-1, 1:-1, 2:],
        arr[1:-1, 1:-1, :-2],
    )


def relax(phi_pad, sig_pad, source):
    centre = sig_pad[1:-1, 1:-1, 1:-1]
    numer = source
    denom = jnp.zeros_like(source) + REACT
    for near_phi, near_sig in zip(beside(phi_pad), beside(sig_pad)):
        face = 0.5 * (centre + near_sig)
        numer = numer + face * near_phi
        denom = denom + face
    return jnp.where(centre > 0.0, numer / denom, 0.0)


def butler(volt, site_rate, tile_press_in, site_live):
    eta = volt - 0.5 * jnp.log(tile_press_in[1] / tile_press_in[0])
    return site_live.astype(jnp.float32) * site_rate * (jnp.exp(0.6 * eta) - jnp.exp(-0.4 * eta))


def diffuse(own, near, throat_count, throat_weight, pore_exchange, pore_current):
    slot = lax.broadcasted_iota(jnp.int32, throat_weight.shape, 0)
    masked = jnp.where(slot < throat_count[None, :], throat_weight, 0.0)
    wsum = jnp.sum(masked, axis=0)
    sum_a = jnp.sum(masked * near[0], axis=0)
    sum_b = jnp.sum(masked * near[1], axis=0)
    mag_a = jnp.abs(own[0])
    mag_b = jnp.abs(own[1])
    total = mag_a + mag_b + 1.0
    diff_a = DK_A / (1.0 + DK_A / DIFF_M * mag_b / total)
    diff_b = DK_B / (1.0 + DK_B / DIFF_M * mag_a / total)
    new_a = (diff_a * sum_a + pore_exchange * BATH_A - CURRENT_SCALE * pore_current) / (
        diff_a * wsum + pore_exchange
    )
    new_b = (diff_b * sum_b + pore_exchange * BATH_B + CURRENT_SCALE * pore_current) / (
        diff_b * wsum + pore_exchange
    )
    return jnp.stack([new_a, new_b])


def table_slot(device, local, own_coords, size_y, size_z, per_dev):
    delta_x = device // (size_y * size_z) - own_coords[0]
    delta_y = device // size_z % size_y - own_coords[1]
    delta_z = device % size_z - own_coords[2]
    return (((delta_x + 1) * 3 + (delta_y + 1)) * 3 + (delta_z + 1)) * per_dev + local


def body(
    labels,
    conduct_scale,
    phase_sigma,
    source,
    potential_in,
    site_voxel,
    site_owner,
    site_pore,
    site_live,
    site_rate,
    tile_press_in,
    throat_nbr,
    throat_count,
    throat_weight,
    pore_exchange,
    pore_press_in,
):
    sigma = conductivity(labels, conduct_scale, phase_sigma)
    sig_pad = extended(sigma, (("gx", 0), ("gy", 1), ("gz", 2)), 1)
    phi = potential_in
    for sweep in range(SWEEPS_E):
        phi_pad = extended(phi, (("gx", 0), ("gy", 1), ("gz", 2)), 1)
        phi = relax(phi_pad, sig_pad, source)
    volt = phi.reshape(-1)[site_voxel]
    current = butler(volt, site_rate, tile_press_in, site_live)
    live_float = site_live.astype(jnp.float32)[None, :]
    size_y = lax.axis_size("gy")
    size_z = lax.axis_size("gz")
    own_coords = (lax.axis_index("gx"), lax.axis_index("gy"), lax.axis_index("gz"))
    pore_total = pore_exchange.shape[0]
    site_slot = table_slot(site_owner, site_pore, own_coords, size_y, size_z, pore_total)
    buckets = (
        jnp.zeros((27 * pore_total,), jnp.float32)
        .at[site_slot]
        .add(current)
        .reshape(3, 3, 3, pore_total)
    )
    beside_all = extended(buckets, (("gx", 0), ("gy", 1), ("gz", 2)), 1)
    pore_current = (
        buckets[1, 1, 1]
        + beside_all[0, 2, 2]
        + beside_all[4, 2, 2]
        + beside_all[2, 0, 2]
        + beside_all[2, 4, 2]
        + beside_all[2, 2, 0]
        + beside_all[2, 2, 4]
    )
    press = pore_press_in
    for sweep in range(SWEEPS_G):
        whole = lax.all_gather(press, ("gx", "gy", "gz"), axis=1, tiled=True)
        near = whole[:, throat_nbr]
        press = diffuse(press, near, throat_count, throat_weight, pore_exchange, pore_current)
    final_table = extended(
        press.reshape(2, 1, 1, 1, pore_total), (("gx", 1), ("gy", 2), ("gz", 3)), 1
    )
    tile_press = final_table.reshape(2, -1)[:, site_slot] * live_float
    return (phi, press, tile_press)


def solution(mesh):
    return jax.shard_map(
        body,
        mesh=mesh,
        in_specs=(
            P("gx", "gy", "gz"),
            P("gx", "gy", "gz"),
            P(),
            P("gx", "gy", "gz"),
            P("gx", "gy", "gz"),
            P(("gx", "gy", "gz")),
            P(("gx", "gy", "gz")),
            P(("gx", "gy", "gz")),
            P(("gx", "gy", "gz")),
            P(("gx", "gy", "gz")),
            P(None, ("gx", "gy", "gz")),
            P(None, ("gx", "gy", "gz")),
            P(("gx", "gy", "gz")),
            P(None, ("gx", "gy", "gz")),
            P(("gx", "gy", "gz")),
            P(None, ("gx", "gy", "gz")),
        ),
        out_specs=(P("gx", "gy", "gz"), P(None, ("gx", "gy", "gz")), P(None, ("gx", "gy", "gz"))),
        check_vma=False,
    )
```

profile of v0, /device:TPU:0, one launch (start us, length us, event | category | flops | bytes accessed | tf_op | source)
XLA Modules:
  0.0 547.9 jit_solution(10086411336683585272)
XLA Ops:
  2.0 6.7 %copy_multiply_fusion = f32[32,32,512]{2,0,1:T(8,128)S(1)} fusion(f32[32,32,512]{2,1,0:T(8,128)} %param.17, s32[32,32,512]{2,1,0:T(8,128)} %param.16, f32[]{:T(128)} %bitcast.2, f32[]{:T(128)} %bitcast.1, f32[]{:T(128)} %bitcast), kind=kLoop, calls=%fused_computation.163 | loop fusion | flops 2621440 | bytes 6291468 | tf_op jit(solution)/shard_map/mul | solution.py:36
  10.1 5.5 collective-permute-start.2
  17.1 5.4 collective-permute-start.3
  25.2 4.6 collective-permute-start.6
  31.8 5.2 collective-permute-start.7
  40.9 4.2 collective-permute-start.10
  50.0 4.2 collective-permute-start.11
  60.5 18.4 %fusion.45 = f32[32,32,512]{2,0,1:T(8,128)S(1)} fusion(f32[34,34,1]{2,0,1:T(8,128)} %copy.86, f32[34,1,512]{2,0,1:T(8,128)} %collective-permute-done.5, f32[34,1,512]{2,0,1:T(8,128)} %collective-permute-done.7, f32[1,32,512]{2,0,1:T(1,128)} %copy-done.10, f32[32,32,512]{2,0,1:T(8,128)} %copy-done.4, f32[1,32,512]{2,0,1:T(1,128)} %copy-done.11, ...), kind=kLoop, calls=%fused_computation.105 | loop fusion | flops 36175872 | bytes 8947776 | tf_op jit(solution)/shard_map/jit(_where)/select_n | solution.py:58
  80.3 5.4 collective-permute-start.13
  89.2 4.4 collective-permute-start.15
  102.5 4.2 collective-permute-start.17
  110.8 18.4 %fusion.31 = f32[32,32,512]{2,0,1:T(8,128)S(1)} fusion(f32[34,34,1]{2,0,1:T(8,128)} %copy.91, f32[34,1,512]{2,0,1:T(8,128)} %copy-done.19, f32[34,1,512]{2,0,1:T(8,128)} %copy-done.21, f32[1,32,512]{2,0,1:T(1,128)} %copy-done.13, f32[32,32,512]{2,0,1:T(8,128)} %copy-done.3, f32[1,32,512]{2,0,1:T(1,128)} %copy-done.15, f32[34,34,1]{2,0,1:T(8,128)} %copy.89, ...), kind=kLoop, calls=%fused_computation.73 | loop fusion | flops 36175872 | bytes 8947776 | tf_op jit(solution)/shard_map/jit(_where)/select_n | solution.py:58
  130.6 5.4 collective-permute-start.19
  139.3 4.9 collective-permute-start.21
  153.2 4.2 collective-permute-start.23
  162.7 18.4 %fusion.17 = f32[32,32,512]{2,0,1:T(8,128)S(1)} fusion(f32[34,34,1]{2,0,1:T(8,128)} %copy.96, f32[34,1,512]{2,0,1:T(8,128)} %copy-done.18, f32[34,1,512]{2,0,1:T(8,128)} %copy-done.20, f32[1,32,512]{2,0,1:T(1,128)} %copy-done.12, f32[32,32,512]{2,0,1:T(8,128)} %copy-done.2, f32[1,32,512]{2,0,1:T(1,128)} %copy-done.14, f32[34,34,1]{2,0,1:T(8,128)} %copy.94, ...), kind=kLoop, calls=%fused_computation.41 | loop fusion | flops 36175872 | bytes 8947776 | tf_op jit(solution)/shard_map/jit(_where)/select_n | solution.py:58
  184.5 6.4 %collective-permute-start.25 = (f32[1,32,512]{2,0,1:T(1,128)}, f32[1,32,512]{2,0,1:T(1,128)}, u32[]{:S(2)}, u32[]{:S(2)}) collective-permute-start(f32[1,32,512]{2,0,1:T(1,128)} %get-tuple-element.42), channel_id=1, source_target_pairs={{0,8},{8,16},{16,24},{1,9},{9,17},{17,25},{2,10},{10,18},{18,26},{... | collective-permute-start | bytes 196616 | tf_op jit(solution)/shard_map/ppermute | solution.py:26
  194.7 4.9 collective-permute-start.27
  216.9 18.4 %fusion.3 = f32[32,32,512]{2,0,1:T(8,128)S(1)} fusion(f32[34,34,1]{2,0,1:T(8,128)} %copy.101, f32[34,1,512]{2,0,1:T(8,128)} %copy-done.16, f32[34,1,512]{2,0,1:T(8,128)} %copy-done.17, f32[1,32,512]{2,0,1:T(1,128)} %collective-permute-done.24, f32[32,32,512]{2,0,1:T(8,128)} %copy-done, f32[1,32,512]{2,0,1:T(1,128)} %collective-permute-done.25, ...), kind=kLoop, calls=%fused_computation.9 | loop fusion | flops 36175872 | bytes 8947776 | tf_op jit(solution)/shard_map/jit(_where)/select_n | solution.py:58
  237.9 6.2 %gather_fusion.1 = f32[1024]{0:T(1024)S(1)} fusion(f32[524288]{0:T(1024)S(1)} %bitcast.49, s32[1024]{0:T(1024)S(1)} %copy-done.29), kind=kCustom, calls=%fused_computation.1 | custom fusion | bytes 12288 | tf_op jit(solution)/shard_map/gather | solution.py:117
  244.1 6.7 %scatter_custom_fusion = f32[13824]{0:T(1024)S(1)} fusion(s32[1024]{0:T(1024)} %get-tuple-element.21, f32[1024]{0:T(1024)S(1)} %subtract_multiply_fusion, f32[]{:T(128)} %constant.74.clone.1), kind=kCustom, calls=%fused_computation.213 | custom fusion | flops 1024 | bytes 55808 | tf_op jit(solution)/shard_map/scatter-add | solution.py:128
  250.9 5.3 collective-permute-start.30
  257.8 5.7 %collective-permute-done.31 = f32[1,3,3,512]{3,2,1,0:T(4,128)S(1)} collective-permute-done((f32[1,3,3,512]{3,2,1,0:T(4,128)S(1)}, f32[1,3,3,512]{3,2,1,0:T(4,128)S(1)}, u32[]{:S(2)}, u32[]{:S(2)}) %collective-permute-start.31) | collective-permute-done | bytes 18464 | tf_op jit(solution)/shard_map/ppermute | solution.py:27
  263.4 4.2 collective-permute-start.32
  269.0 108.7 %all_gather.6 = f32[2,16384]{0,1:T(8,128)} all-gather(f32[2,512]{0,1:T(8,128)S(1)} %copy.102), channel_id=1, replica_groups=mesh['gx'=4,'gy'=4,'gz'=2] {'gx','gy','gz'}, dimensions={1}, use_global_device_ids=true | all-gather | bytes 135168 | tf_op jit(solution)/shard_map/all_gather | solution.py:143
  377.7 14.2 %gather_fusion = f32[4096,2]{1,0:T(8,128)S(1)} fusion(f32[2,16384]{0,1:T(8,128)} %all_gather.6, s32[4096]{0:T(1024)S(1)} %copy-done.22), kind=kCustom, calls=%fused_computation | custom fusion | bytes 81920 | tf_op jit(solution)/shard_map/gather | solution.py:144
  398.2 105.5 %all_gather.7 = f32[2,16384]{0,1:T(8,128)} all-gather(f32[2,512]{0,1:T(8,128)S(1)} %copy.105), channel_id=1, replica_groups=mesh['gx'=4,'gy'=4,'gz'=2] {'gx','gy','gz'}, dimensions={1}, use_global_device_ids=true | all-gather | bytes 135168 | tf_op jit(solution)/shard_map/all_gather | solution.py:143
  503.7 14.1 %gather_fusion.2 = f32[4096,2]{1,0:T(8,128)S(1)} fusion(f32[2,16384]{0,1:T(8,128)} %all_gather.7, s32[4096]{0:T(1024)S(1)} %copy-done.22), kind=kCustom, calls=%fused_computation.2 | custom fusion | bytes 81920 | tf_op jit(solution)/shard_map/gather | solution.py:144
  521.2 4.2 collective-permute-done.37
  528.1 4.2 collective-permute-done.39
  536.8 4.3 copy.107
  541.0 5.8 %gather_fusion.3 = f32[1024,2]{1,0:T(8,128)S(1)} fusion(f32[2,13824]{0,1:T(8,128)} %bitcast.51, s32[1024]{0:T(1024)S(1)} %copy-done.26), kind=kCustom, calls=%fused_computation.3 | custom fusion | bytes 20480 | tf_op jit(solution)/shard_map/gather | solution.py:149
  (212 shorter events, 107.8 us)
Async XLA Ops:
  8.8 15.0 %collective-permute-start = (f32[1,32,512]{2,0,1:T(1,128)S(1)}, f32[1,32,512]{2,0,1:T(1,128)S(1)}, u32[]{:S(2)}, u32[]{:S(2)}) collective-permute-start(f32[1,32,512]{2,0,1:T(1,128)S(1)} %get-tuple-element.49), channel_id=1, source_target_pairs={{8,0},{16,8},{24,16},{9,1},{17,9},{25,17},{10,2},{18,10},{26,18},{... | collective-permute-start | bytes 196616 | tf_op jit(solution)/shard_map/ppermute | solution.py:27
  10.1 13.7 %collective-permute-start.2 = (f32[1,32,512]{2,0,1:T(1,128)S(1)}, f32[1,32,512]{2,0,1:T(1,128)S(1)}, u32[]{:S(2)}, u32[]{:S(2)}) collective-permute-start(f32[1,32,512]{2,0,1:T(1,128)S(1)} %get-tuple-element.48), channel_id=1, source_target_pairs={{0,8},{8,16},{16,24},{1,9},{9,17},{17,25},{2,10},{10,18},{18,26},{... | collective-permute-start | bytes 196616 | tf_op jit(solution)/shard_map/ppermute | solution.py:26
  15.7 14.0 %collective-permute-start.1 = (f32[1,32,512]{2,0,1:T(1,128)S(1)}, f32[1,32,512]{2,0,1:T(1,128)S(1)}, u32[]{:S(2)}, u32[]{:S(2)}) collective-permute-start(f32[1,32,512]{2,0,1:T(1,128)S(1)} %copy.73), channel_id=1, source_target_pairs={{8,0},{16,8},{24,16},{9,1},{17,9},{25,17},{10,2},{18,10},{26,18},{... | collective-permute-start | bytes 196616 | tf_op jit(solution)/shard_map/ppermute | solution.py:27
  17.1 12.6 %collective-permute-start.3 = (f32[1,32,512]{2,0,1:T(1,128)S(1)}, f32[1,32,512]{2,0,1:T(1,128)S(1)}, u32[]{:S(2)}, u32[]{:S(2)}) collective-permute-start(f32[1,32,512]{2,0,1:T(1,128)S(1)} %copy.76), channel_id=1, source_target_pairs={{0,8},{8,16},{16,24},{1,9},{9,17},{17,25},{2,10},{10,18},{18,26},{... | collective-permute-start | bytes 196616 | tf_op jit(solution)/shard_map/ppermute | solution.py:26
  23.9 13.1 %collective-permute-start.4 = (f32[34,1,512]{2,0,1:T(8,128)S(1)}, f32[34,1,512]{2,0,1:T(8,128)S(1)}, u32[]{:S(2)}, u32[]{:S(2)}) collective-permute-start(f32[34,1,512]{2,0,1:T(8,128)S(1)} %get-tuple-element.39), channel_id=1, source_target_pairs={{2,0},{4,2},{6,4},{3,1},{5,3},{7,5},{10,8},{12,10},{14,12},{11,9},... | collective-permute-start | bytes 208904 | tf_op jit(solution)/shard_map/ppermute | solution.py:27
  25.2 11.8 %collective-permute-start.6 = (f32[34,1,512]{2,0,1:T(8,128)S(1)}, f32[34,1,512]{2,0,1:T(8,128)S(1)}, u32[]{:S(2)}, u32[]{:S(2)}) collective-permute-start(f32[34,1,512]{2,0,1:T(8,128)S(1)} %get-tuple-element.38), channel_id=1, source_target_pairs={{0,2},{2,4},{4,6},{1,3},{3,5},{5,7},{8,10},{10,12},{12,14},{9,11},... | collective-permute-start | bytes 208904 | tf_op jit(solution)/shard_map/ppermute | solution.py:26
  30.5 14.6 %collective-permute-start.5 = (f32[34,1,512]{2,0,1:T(8,128)}, f32[34,1,512]{2,0,1:T(8,128)}, u32[]{:S(2)}, u32[]{:S(2)}) collective-permute-start(f32[34,1,512]{2,0,1:T(8,128)} %get-tuple-element.41), channel_id=1, source_target_pairs={{2,0},{4,2},{6,4},{3,1},{5,3},{7,5},{10,8},{12,10},{14,12},{11,9},... | collective-permute-start | bytes 208904 | tf_op jit(solution)/shard_map/ppermute | solution.py:27
  31.8 13.3 %collective-permute-start.7 = (f32[34,1,512]{2,0,1:T(8,128)}, f32[34,1,512]{2,0,1:T(8,128)}, u32[]{:S(2)}, u32[]{:S(2)}) collective-permute-start(f32[34,1,512]{2,0,1:T(8,128)} %get-tuple-element.40), channel_id=1, source_target_pairs={{0,2},{2,4},{4,6},{1,3},{3,5},{5,7},{8,10},{10,12},{12,14},{9,11},... | collective-permute-start | bytes 208904 | tf_op jit(solution)/shard_map/ppermute | solution.py:26
  38.6 15.6 %collective-permute-start.8 = (f32[34,34,1]{1,0,2:T(8,128)}, f32[34,34,1]{1,0,2:T(8,128)}, u32[]{:S(2)}, u32[]{:S(2)}) collective-permute-start(f32[34,34,1]{1,0,2:T(8,128)} %copy.79), channel_id=1, source_target_pairs={{1,0},{3,2},{5,4},{7,6},{9,8},{11,10},{13,12},{15,14},{17,16},{19,... | collective-permute-start | bytes 13880 | tf_op jit(solution)/shard_map/ppermute | solution.py:27
  40.9 14.5 %collective-permute-start.10 = (f32[34,34,1]{1,0,2:T(8,128)}, f32[34,34,1]{1,0,2:T(8,128)}, u32[]{:S(2)}, u32[]{:S(2)}) collective-permute-start(f32[34,34,1]{1,0,2:T(8,128)} %copy.83), channel_id=1, source_target_pairs={{0,1},{2,3},{4,5},{6,7},{8,9},{10,11},{12,13},{14,15},{16,17},{18,... | collective-permute-start | bytes 13880 | tf_op jit(solution)/shard_map/ppermute | solution.py:26
  47.7 8.8 %collective-permute-start.9 = (f32[34,34,1]{1,0,2:T(8,128)}, f32[34,34,1]{1,0,2:T(8,128)}, u32[]{:S(2)}, u32[]{:S(2)}) collective-permute-start(f32[34,34,1]{1,0,2:T(8,128)} %copy.81), channel_id=1, source_target_pairs={{1,0},{3,2},{5,4},{7,6},{9,8},{11,10},{13,12},{15,14},{17,16},{19,... | collective-permute-start | bytes 13880 | tf_op jit(solution)/shard_map/ppermute | solution.py:27
  50.0 8.5 %collective-permute-start.11 = (f32[34,34,1]{1,0,2:T(8,128)}, f32[34,34,1]{1,0,2:T(8,128)}, u32[]{:S(2)}, u32[]{:S(2)}) collective-permute-start(f32[34,34,1]{1,0,2:T(8,128)} %copy.85), channel_id=1, source_target_pairs={{0,1},{2,3},{4,5},{6,7},{8,9},{10,11},{12,13},{14,15},{16,17},{18,... | collective-permute-start | bytes 13880 | tf_op jit(solution)/shard_map/ppermute | solution.py:26
  79.0 7.1 %collective-permute-start.12 = (f32[1,32,512]{2,0,1:T(1,128)S(1)}, f32[1,32,512]{2,0,1:T(1,128)S(1)}, u32[]{:S(2)}, u32[]{:S(2)}) collective-permute-start(f32[1,32,512]{2,0,1:T(1,128)S(1)} %get-tuple-element.47), channel_id=1, source_target_pairs={{8,0},{16,8},{24,16},{9,1},{17,9},{25,17},{10,2},{18,10},{26,18},{... | collective-permute-start | bytes 196616 | tf_op jit(solution)/shard_map/ppermute | solution.py:27
  80.3 7.3 %collective-permute-start.13 = (f32[1,32,512]{2,0,1:T(1,128)S(1)}, f32[1,32,512]{2,0,1:T(1,128)S(1)}, u32[]{:S(2)}, u32[]{:S(2)}) collective-permute-start(f32[1,32,512]{2,0,1:T(1,128)S(1)} %get-tuple-element.46), channel_id=1, source_target_pairs={{0,8},{8,16},{16,24},{1,9},{9,17},{17,25},{2,10},{10,18},{18,26},{... | collective-permute-start | bytes 196616 | tf_op jit(solution)/shard_map/ppermute | solution.py:26
  87.7 6.3 %collective-permute-start.14 = (f32[34,1,512]{2,0,1:T(8,128)S(1)}, f32[34,1,512]{2,0,1:T(8,128)S(1)}, u32[]{:S(2)}, u32[]{:S(2)}) collective-permute-start(f32[34,1,512]{2,0,1:T(8,128)S(1)} %get-tuple-element.37), channel_id=1, source_target_pairs={{2,0},{4,2},{6,4},{3,1},{5,3},{7,5},{10,8},{12,10},{14,12},{11,9},... | collective-permute-start | bytes 208904 | tf_op jit(solution)/shard_map/ppermute | solution.py:27
  89.2 6.4 %collective-permute-start.15 = (f32[34,1,512]{2,0,1:T(8,128)S(1)}, f32[34,1,512]{2,0,1:T(8,128)S(1)}, u32[]{:S(2)}, u32[]{:S(2)}) collective-permute-start(f32[34,1,512]{2,0,1:T(8,128)S(1)} %get-tuple-element.36), channel_id=1, source_target_pairs={{0,2},{2,4},{4,6},{1,3},{3,5},{5,7},{8,10},{10,12},{12,14},{9,11},... | collective-permute-start | bytes 208904 | tf_op jit(solution)/shard_map/ppermute | solution.py:26
  99.2 7.6 %collective-permute-start.16 = (f32[34,34,1]{1,0,2:T(8,128)}, f32[34,34,1]{1,0,2:T(8,128)}, u32[]{:S(2)}, u32[]{:S(2)}) collective-permute-start(f32[34,34,1]{1,0,2:T(8,128)} %copy.88), channel_id=1, source_target_pairs={{1,0},{3,2},{5,4},{7,6},{9,8},{11,10},{13,12},{15,14},{17,16},{19,... | collective-permute-start | bytes 13880 | tf_op jit(solution)/shard_map/ppermute | solution.py:27
  129.3 7.1 %collective-permute-start.18 = (f32[1,32,512]{2,0,1:T(1,128)S(1)}, f32[1,32,512]{2,0,1:T(1,128)S(1)}, u32[]{:S(2)}, u32[]{:S(2)}) collective-permute-start(f32[1,32,512]{2,0,1:T(1,128)S(1)} %get-tuple-element.45), channel_id=1, source_target_pairs={{8,0},{16,8},{24,16},{9,1},{17,9},{25,17},{10,2},{18,10},{26,18},{... | collective-permute-start | bytes 196616 | tf_op jit(solution)/shard_map/ppermute | solution.py:27
  130.6 7.3 %collective-permute-start.19 = (f32[1,32,512]{2,0,1:T(1,128)S(1)}, f32[1,32,512]{2,0,1:T(1,128)S(1)}, u32[]{:S(2)}, u32[]{:S(2)}) collective-permute-start(f32[1,32,512]{2,0,1:T(1,128)S(1)} %get-tuple-element.44), channel_id=1, source_target_pairs={{0,8},{8,16},{16,24},{1,9},{9,17},{17,25},{2,10},{10,18},{18,26},{... | collective-permute-start | bytes 196616 | tf_op jit(solution)/shard_map/ppermute | solution.py:26
  138.0 6.7 %collective-permute-start.20 = (f32[34,1,512]{2,0,1:T(8,128)S(1)}, f32[34,1,512]{2,0,1:T(8,128)S(1)}, u32[]{:S(2)}, u32[]{:S(2)}) collective-permute-start(f32[34,1,512]{2,0,1:T(8,128)S(1)} %get-tuple-element.35), channel_id=1, source_target_pairs={{2,0},{4,2},{6,4},{3,1},{5,3},{7,5},{10,8},{12,10},{14,12},{11,9},... | collective-permute-start | bytes 208904 | tf_op jit(solution)/shard_map/ppermute | solution.py:27
  139.3 7.0 %collective-permute-start.21 = (f32[34,1,512]{2,0,1:T(8,128)S(1)}, f32[34,1,512]{2,0,1:T(8,128)S(1)}, u32[]{:S(2)}, u32[]{:S(2)}) collective-permute-start(f32[34,1,512]{2,0,1:T(8,128)S(1)} %get-tuple-element.34), channel_id=1, source_target_pairs={{0,2},{2,4},{4,6},{1,3},{3,5},{5,7},{8,10},{10,12},{12,14},{9,11},... | collective-permute-start | bytes 208904 | tf_op jit(solution)/shard_map/ppermute | solution.py:26
  149.8 8.9 %collective-permute-start.22 = (f32[34,34,1]{1,0,2:T(8,128)}, f32[34,34,1]{1,0,2:T(8,128)}, u32[]{:S(2)}, u32[]{:S(2)}) collective-permute-start(f32[34,34,1]{1,0,2:T(8,128)} %copy.93), channel_id=1, source_target_pairs={{1,0},{3,2},{5,4},{7,6},{9,8},{11,10},{13,12},{15,14},{17,16},{19,... | collective-permute-start | bytes 13880 | tf_op jit(solution)/shard_map/ppermute | solution.py:27
  153.2 7.6 %collective-permute-start.23 = (f32[34,34,1]{1,0,2:T(8,128)}, f32[34,34,1]{1,0,2:T(8,128)}, u32[]{:S(2)}, u32[]{:S(2)}) collective-permute-start(f32[34,34,1]{1,0,2:T(8,128)} %copy.95), channel_id=1, source_target_pairs={{0,1},{2,3},{4,5},{6,7},{8,9},{10,11},{12,13},{14,15},{16,17},{18,... | collective-permute-start | bytes 13880 | tf_op jit(solution)/shard_map/ppermute | solution.py:26
  183.2 8.3 %collective-permute-start.24 = (f32[1,32,512]{2,0,1:T(1,128)}, f32[1,32,512]{2,0,1:T(1,128)}, u32[]{:S(2)}, u32[]{:S(2)}) collective-permute-start(f32[1,32,512]{2,0,1:T(1,128)} %get-tuple-element.43), channel_id=1, source_target_pairs={{8,0},{16,8},{24,16},{9,1},{17,9},{25,17},{10,2},{18,10},{26,18},{... | collective-permute-start | bytes 196616 | tf_op jit(solution)/shard_map/ppermute | solution.py:27
  184.5 8.0 %collective-permute-start.25 = (f32[1,32,512]{2,0,1:T(1,128)}, f32[1,32,512]{2,0,1:T(1,128)}, u32[]{:S(2)}, u32[]{:S(2)}) collective-permute-start(f32[1,32,512]{2,0,1:T(1,128)} %get-tuple-element.42), channel_id=1, source_target_pairs={{0,8},{8,16},{16,24},{1,9},{9,17},{17,25},{2,10},{10,18},{18,26},{... | collective-permute-start | bytes 196616 | tf_op jit(solution)/shard_map/ppermute | solution.py:26
  193.4 6.9 %collective-permute-start.26 = (f32[34,1,512]{2,0,1:T(8,128)S(1)}, f32[34,1,512]{2,0,1:T(8,128)S(1)}, u32[]{:S(2)}, u32[]{:S(2)}) collective-permute-start(f32[34,1,512]{2,0,1:T(8,128)S(1)} %get-tuple-element.33), channel_id=1, source_target_pairs={{2,0},{4,2},{6,4},{3,1},{5,3},{7,5},{10,8},{12,10},{14,12},{11,9},... | collective-permute-start | bytes 208904 | tf_op jit(solution)/shard_map/ppermute | solution.py:27
  194.7 7.0 %collective-permute-start.27 = (f32[34,1,512]{2,0,1:T(8,128)S(1)}, f32[34,1,512]{2,0,1:T(8,128)S(1)}, u32[]{:S(2)}, u32[]{:S(2)}) collective-permute-start(f32[34,1,512]{2,0,1:T(8,128)S(1)} %get-tuple-element.32), channel_id=1, source_target_pairs={{0,2},{2,4},{4,6},{1,3},{3,5},{5,7},{8,10},{10,12},{12,14},{9,11},... | collective-permute-start | bytes 208904 | tf_op jit(solution)/shard_map/ppermute | solution.py:26
  206.0 6.9 %collective-permute-start.29 = (f32[34,34,1]{1,0,2:T(8,128)}, f32[34,34,1]{1,0,2:T(8,128)}, u32[]{:S(2)}, u32[]{:S(2)}) collective-permute-start(f32[34,34,1]{1,0,2:T(8,128)} %copy.100), channel_id=1, source_target_pairs={{0,1},{2,3},{4,5},{6,7},{8,9},{10,11},{12,13},{14,15},{16,17},{18,... | collective-permute-start | bytes 13880 | tf_op jit(solution)/shard_map/ppermute | solution.py:26
  250.9 6.8 %collective-permute-start.30 = (f32[1,3,3,512]{3,2,1,0:T(4,128)S(1)}, f32[1,3,3,512]{3,2,1,0:T(4,128)S(1)}, u32[]{:S(2)}, u32[]{:S(2)}) collective-permute-start(f32[1,3,3,512]{3,2,1,0:T(4,128)S(1)} %slice.392), channel_id=1, source_target_pairs={{0,8},{8,16},{16,24},{1,9},{9,17},{17,25},{2,10},{10,18},{18,26},{... | collective-permute-start | bytes 55304 | tf_op jit(solution)/shard_map/ppermute | solution.py:26
  256.4 7.0 %collective-permute-start.31 = (f32[1,3,3,512]{3,2,1,0:T(4,128)S(1)}, f32[1,3,3,512]{3,2,1,0:T(4,128)S(1)}, u32[]{:S(2)}, u32[]{:S(2)}) collective-permute-start(f32[1,3,3,512]{3,2,1,0:T(4,128)S(1)} %slice.395), channel_id=1, source_target_pairs={{8,0},{16,8},{24,16},{9,1},{17,9},{25,17},{10,2},{18,10},{26,18},{... | collective-permute-start | bytes 55304 | tf_op jit(solution)/shard_map/ppermute | solution.py:27
  263.4 129.0 %collective-permute-start.32 = (f32[5,1,3,512]{3,2,1,0:T(4,128)S(1)}, f32[5,1,3,512]{3,2,1,0:T(4,128)S(1)}, u32[]{:S(2)}, u32[]{:S(2)}) collective-permute-start(f32[5,1,3,512]{3,2,1,0:T(4,128)S(1)} %get-tuple-element.54), channel_id=1, source_target_pairs={{0,2},{2,4},{4,6},{1,3},{3,5},{5,7},{8,10},{10,12},{12,14},{9,11},... | collective-permute-start | bytes 92168 | tf_op jit(solution)/shard_map/ppermute | solution.py:26
  267.7 124.8 %collective-permute-start.33 = (f32[5,1,3,512]{3,2,1,0:T(4,128)S(1)}, f32[5,1,3,512]{3,2,1,0:T(4,128)S(1)}, u32[]{:S(2)}, u32[]{:S(2)}) collective-permute-start(f32[5,1,3,512]{3,2,1,0:T(4,128)S(1)} %get-tuple-element.55), channel_id=1, source_target_pairs={{2,0},{4,2},{6,4},{3,1},{5,3},{7,5},{10,8},{12,10},{14,12},{11,9},... | collective-permute-start | bytes 92168 | tf_op jit(solution)/shard_map/ppermute | solution.py:27
  (46 other events, 455.6 us)
where the time goes:
time: 550 us; the launch traced here: 548 us
  blocking collectives  214 us (39%)
  starting transfers between devices  114 us (21%)
  other arithmetic  100 us (18%)
  local copies, waits for them, and re-layouts  90.3 us (16%)
  waiting for transfers between devices  27.4 us (5%)
    all_gather x2, blocking collectives, body(): whole = lax.all_gather(press, ('gx', 'gy', 'gz'), axis=1, tiled=True)  214 us
    ppermute x21, starting transfers between devices, extended(): before = lax.ppermute(last, axis, up)  86.8 us
    select_n x4, other arithmetic, relax(): return jnp.where(centre > 0.0, numer / denom, 0.0)  73.6 us
    gather x4, local copies, waits for them, and re-layouts, body(): near = whole[:, throat_nbr]  29.6 us
    ppermute x21, starting transfers between devices, extended(): after = lax.ppermute(leading, axis, down)  27.2 us
    ppermute x21, waiting for transfers between devices, extended(): after = lax.ppermute(leading, axis, down)  18.6 us
  transfers between devices with their start and end apart: 42, of which 16 were waited for; matrix products, arithmetic and copies ran while one was open for 8% of the time, Pallas kernels for 0%

commit v1 on v0

v1 whole, which is shorter than its diff:
```python
import functools

import jax
import jax.numpy as jnp
from jax import lax
from jax.experimental import pallas as pl
from jax.experimental.pallas import tpu as pltpu
from jax.sharding import PartitionSpec as P

SWEEPS_E = 4
SWEEPS_G = 2
REACT = 0.1
DK_A = 2.0
DK_B = 0.7
DIFF_M = 1.0
BATH_A = 1.0
BATH_B = 0.2
CURRENT_SCALE = 0.25

LANES = 128
CHUNKS = 4
ORDER = (0, 3, 1, 2)
SLOTS = 7
MESH = pl.DeviceIdType.MESH


def up_z(v, after):
    ext = jnp.concatenate([v, after], axis=1)
    return pltpu.roll(ext, ext.shape[1] - 1, 1)[:, : v.shape[1]]


def down_z(v, before):
    ext = jnp.concatenate([before, v], axis=1)
    return pltpu.roll(ext, 1, 1)[:, before.shape[1] :]


def up_y(v, row, is_last):
    return jnp.where(is_last, row, pltpu.roll(v, v.shape[0] - 1, 0))


def down_y(v, row, is_first):
    return jnp.where(is_first, row, pltpu.roll(v, 1, 0))


def kernel(
    sizes,
    table_ref,
    lab_hbm,
    cs_hbm,
    src_hbm,
    phi_hbm,
    voxel_ref,
    owner_ref,
    spore_ref,
    live_ref,
    rate_ref,
    tpress_ref,
    nbr_ref,
    count_ref,
    weight_ref,
    exch_ref,
    press_ref,
    phi_out,
    press_out,
    tile_out,
    lab,
    cs,
    src,
    sig,
    phi0,
    phi1,
    phi2,
    phi3,
    fin,
    gxf,
    gyf,
    gzf,
    inv,
    ylo,
    yhi,
    ysend_lo,
    ysend_hi,
    zlo,
    zhi,
    onehot,
    tab0,
    tab1,
    tab2,
    bucket,
    arrived,
    load_sem,
    out_sem,
    xs_sem,
    xr_sem,
    ys_sem,
    yr_sem,
    zs_sem,
    zr_sem,
    ps_sem,
    pr_sem,
):
    size_x, size_y, size_z = sizes
    nx, ny, nz = src.shape
    nc = nx // CHUNKS
    pores = press_ref.shape[1]
    segs = pores // LANES
    ix, iy, iz = (lax.axis_index("gx"), lax.axis_index("gy"), lax.axis_index("gz"))

    axes = (("gx", ix, size_x), ("gy", iy, size_y), ("gz", iz, size_z))
    there = []
    where_to = []
    for name, at, size in axes:
        there += [at > 0, at < size - 1]
        where_to += [{name: at - 1}, {name: at + 1}]

    def load(which, chunk):
        rows = pl.ds(chunk * nc, nc)
        far, near = ((lab_hbm, lab), (cs_hbm, cs), (phi_hbm, phi0), (src_hbm, src))[which]
        inner = pl.ds(1 + chunk * nc, nc) if which == 2 else rows
        return pltpu.make_async_copy(far.at[rows], near.at[inner], load_sem.at[which, chunk])

    for part in ((0, 1), (2,), (3,)):
        for chunk in ORDER:
            for which in part:
                load(which, chunk).start()

    barrier = pltpu.get_barrier_semaphore()
    total = jnp.int32(0)
    for k in range(6):
        total = total + there[k].astype(jnp.int32)

        @pl.when(there[k])
        def _():
            pl.semaphore_signal(barrier, inc=1, device_id=where_to[k], device_id_type=MESH)

    fields = (sig, phi0, phi1, phi2, phi3)

    def x_copy(e, side):
        field = fields[e]
        return pltpu.make_async_remote_copy(
            src_ref=field.at[1 if side == 0 else nx],
            dst_ref=field.at[nx + 1 if side == 0 else 0],
            send_sem=xs_sem.at[e, side],
            recv_sem=xr_sem.at[e, 1 - side],
            device_id=where_to[side],
            device_id_type=MESH,
        )

    def y_copy(e, side, chunk):
        rows = pl.ds(chunk * nc, nc)
        return pltpu.make_async_remote_copy(
            src_ref=(ysend_lo if side == 0 else ysend_hi).at[e, rows],
            dst_ref=(yhi if side == 0 else ylo).at[e, rows],
            send_sem=ys_sem.at[e, side, chunk],
            recv_sem=yr_sem.at[e, 1 - side, chunk],
            device_id=where_to[2 + side],
            device_id_type=MESH,
        )

    def z_copy(e, side, chunk):
        return pltpu.make_async_remote_copy(
            src_ref=fields[e].at[
                pl.ds(1 + chunk * nc, nc), :, pl.ds(0 if side == 0 else nz - LANES, LANES)
            ],
            dst_ref=(zhi if side == 0 else zlo).at[e, pl.ds(chunk * nc, nc)],
            send_sem=zs_sem.at[e, side, chunk],
            recv_sem=zr_sem.at[e, 1 - side, chunk],
            device_id=where_to[4 + side],
            device_id_type=MESH,
        )

    tabs = (tab0, tab1, tab2)

    def p_copy(e, k):
        opposite = 1 + (k ^ 1)
        return pltpu.make_async_remote_copy(
            src_ref=tabs[e].at[0] if e < 3 else bucket.at[1 + k],
            dst_ref=tabs[e].at[opposite] if e < 3 else arrived.at[opposite],
            send_sem=ps_sem.at[e, k],
            recv_sem=pr_sem.at[e, k ^ 1],
            device_id=where_to[k],
            device_id_type=MESH,
        )


    def send_faces(e, chunk):
        if chunk == 0:

            @pl.when(there[0])
            def _():
                x_copy(e, 0).start()

        if chunk == CHUNKS - 1:

            @pl.when(there[1])
            def _():
                x_copy(e, 1).start()

        for side in (0, 1):

            @pl.when(there[2 + side])
            def _():
                y_copy(e, side, chunk).start()

            @pl.when(there[4 + side])
            def _():
                z_copy(e, side, chunk).start()

    def await_faces(e, chunk):
        if chunk == 0:

            @pl.when(there[0])
            def _():
                x_copy(e, 1).wait_recv()

        if chunk == CHUNKS - 1:

            @pl.when(there[1])
            def _():
                x_copy(e, 0).wait_recv()

        for side in (0, 1):

            @pl.when(there[2 + side])
            def _():
                y_copy(e, 1 - side, chunk).wait_recv()

            @pl.when(there[4 + side])
            def _():
                z_copy(e, 1 - side, chunk).wait_recv()

    def send_pores(e):
        for k in range(6):

            @pl.when(there[k])
            def _():
                p_copy(e, k).start()

    def await_pores(e):
        for k in range(6):

            @pl.when(there[k])
            def _():
                p_copy(e, k ^ 1).wait_recv()

    for side, (xat, ybuf, zbuf) in enumerate(((0, ylo, zlo), (nx + 1, yhi, zhi))):

        @pl.when(jnp.logical_not(there[side]))
        def _():
            for field in fields:
                field[xat] = jnp.zeros((ny, nz), jnp.float32)

        @pl.when(jnp.logical_not(there[2 + side]))
        def _():
            ybuf[...] = jnp.zeros(ybuf.shape, jnp.float32)

        @pl.when(jnp.logical_not(there[4 + side]))
        def _():
            for e in range(5):

                def clear(i, carry):
                    zbuf[e, i] = jnp.zeros((ny, LANES), jnp.float32)
                    return carry

                lax.fori_loop(0, nx, clear, 0)

    for k in range(6):

        @pl.when(jnp.logical_not(there[k]))
        def _():
            for tab in tabs:
                tab[1 + k] = jnp.zeros((2, pores), jnp.float32)
            arrived[1 + k] = jnp.zeros((1, pores), jnp.float32)

    tab0[0] = press_ref[...]

    pl.semaphore_wait(barrier, total)
    send_pores(0)

    s0, s1, s2 = (table_ref[0], table_ref[1], table_ref[2])
    for chunk in ORDER:
        load(0, chunk).wait()
        load(1, chunk).wait()

        def conductivity(i, carry):
            kind = lab[i]
            value = cs[i] * jnp.where(kind == 0, s0, jnp.where(kind == 1, s1, s2))
            sig[i + 1] = value
            ysend_lo[0, i] = value[0:1]
            ysend_hi[0, i] = value[ny - 1 : ny]
            return carry

        lax.fori_loop(chunk * nc, (chunk + 1) * nc, conductivity, 0)
        send_faces(0, chunk)
    for chunk in ORDER:
        load(2, chunk).wait()

        def pack(i, carry):
            ysend_lo[1, i] = phi0[i + 1, 0:1]
            ysend_hi[1, i] = phi0[i + 1, ny - 1 : ny]
            return carry

        lax.fori_loop(chunk * nc, (chunk + 1) * nc, pack, 0)
        send_faces(1, chunk)

    own = (ix * size_y + iy) * size_z + iz
    bits = pores.bit_length() - 1
    lane_bits = LANES.bit_length() - 1

    def place(device, local):
        delta = device - own
        slot = jnp.zeros(delta.shape, jnp.int32)
        for k, step in enumerate(
            (-size_y * size_z, size_y * size_z, -size_z, size_z, -1, 1)
        ):
            slot = jnp.where(delta == step, k + 1, slot)
        return slot, slot * segs + (local >> lane_bits), local & (LANES - 1)

    nbr = nbr_ref[...]
    _, near_key, near_lane = place(nbr >> bits, nbr & (pores - 1))
    site_pore = spore_ref[...]
    site_slot, site_key, site_lane = place(owner_ref[...], site_pore)
    live = live_ref[...].astype(jnp.float32)
    slot_no = lax.broadcasted_iota(jnp.int32, weight_ref.shape, 0)
    masked = jnp.where(slot_no < count_ref[...], weight_ref[...], 0.0)
    wsum = jnp.sum(masked, axis=0, keepdims=True)
    exch = exch_ref[...]
    pore_no = lax.broadcasted_iota(jnp.int32, (pores, LANES), 0)
    site_rows = site_pore.shape[0]
    for r in range(site_rows):
        hit = jnp.where(pore_no == site_pore[r : r + 1], 1.0, 0.0)
        onehot[:, r * LANES : (r + 1) * LANES] = hit.astype(jnp.bfloat16)

    y_no = lax.broadcasted_iota(jnp.int32, (ny, nz), 0)
    y_first = y_no == 0
    y_last = y_no == ny - 1

    for sweep in range(SWEEPS_E):
        old = fields[1 + sweep]
        last = sweep == SWEEPS_E - 1
        e = 1 + sweep
        for chunk in ORDER:
            if sweep == 0:
                await_faces(0, chunk)
                load(3, chunk).wait()
            await_faces(e, chunk)

            def relax(i, carry):
                phi = old[i + 1]
                if sweep == 0:
                    s = sig[i + 1]
                    g_below = 0.5 * (sig[i] + s)
                    g_above = 0.5 * (s + sig[i + 2])
                    gy = 0.5 * (s + up_y(s, yhi[0, i], y_last))
                    gz = 0.5 * (s + up_z(s, zhi[0, i]))
                    y_low = 0.5 * (ylo[0, i] + s[0:1])
                    gxf[i] = g_below
                    gxf[i + 1] = g_above
                    gyf[i] = gy
                    gzf[i] = gz
                    z_low = 0.5 * (zlo[0, i] + pltpu.roll(s[:, :LANES], LANES - 1, 1))
                    ylo[0, i] = y_low
                    zlo[0, i] = z_low
                    denom = (
                        REACT
                        + g_below
                        + g_above
                        + gy
                        + down_y(gy, y_low, y_first)
                        + gz
                        + down_z(gz, z_low)
                    )
                    scale = jnp.where(s > 0.0, 1.0 / denom, 0.0)
                    inv[i] = scale
                else:
                    g_below = gxf[i]
                    g_above = gxf[i + 1]
                    gy = gyf[i]
                    gz = gzf[i]
                    y_low = ylo[0, i]
                    z_low = zlo[0, i]
                    scale = inv[i]
                numer = (
                    src[i]
                    + g_below * old[i]
                    + g_above * old[i + 2]
                    + gy * up_y(phi, yhi[e, i], y_last)
                    + down_y(gy * phi, y_low * ylo[e, i], y_first)
                    + gz * up_z(phi, zhi[e, i])
                    + down_z(gz * phi, z_low * zlo[e, i])
                )
                value = numer * scale
                if last:
                    fin[i] = value
                else:
                    fields[e + 1][i + 1] = value
                    ysend_lo[e + 1, i] = value[0:1]
                    ysend_hi[e + 1, i] = value[ny - 1 : ny]
                return carry

            lax.fori_loop(chunk * nc, (chunk + 1) * nc, relax, 0)
            if last:
                rows = pl.ds(chunk * nc, nc)
                pltpu.make_async_copy(fin.at[rows], phi_out.at[rows], out_sem.at[chunk]).start()
            else:
                send_faces(e + 1, chunk)

    voxel = voxel_ref[...]
    y_bits, z_bits = (ny.bit_length() - 1, nz.bit_length() - 1)
    vz = voxel & (nz - 1)
    vy = (voxel >> z_bits) & (ny - 1)
    vx = voxel >> (z_bits + y_bits)
    y_tiles, z_tiles = (ny // 8, nz // LANES)
    tile_no = (vx * y_tiles + (vy >> 3)) * z_tiles + (vz >> lane_bits)
    sub = lax.broadcasted_iota(jnp.int32, (8, LANES), 0)

    def spread(a, r):
        return jnp.broadcast_to(a[r : r + 1], (8, LANES))

    tile_rows = [spread(tile_no, r) for r in range(site_rows)]
    lane_rows = [spread(vz & (LANES - 1), r) for r in range(site_rows)]

    def pick(i, accs):
        accs = list(accs)
        for ty in range(y_tiles):
            for tz in range(z_tiles):
                block = fin[i, ty * 8 : ty * 8 + 8, tz * LANES : (tz + 1) * LANES]
                here = (i * y_tiles + ty) * z_tiles + tz
                for r in range(site_rows):
                    got = jnp.take_along_axis(block, lane_rows[r], axis=1)
                    accs[r] = jnp.where(tile_rows[r] == here, got, accs[r])
        return tuple(accs)

    zero = jnp.zeros((8, LANES), jnp.float32)
    accs = lax.fori_loop(0, nx, pick, (zero,) * site_rows)
    volt = jnp.concatenate(
        [
            jnp.sum(jnp.where(sub == spread(vy & 7, r), accs[r], 0.0), axis=0, keepdims=True)
            for r in range(site_rows)
        ],
        axis=0,
    )
    ratio = tpress_ref[1:2, :] / tpress_ref[0:1, :]
    ratio = jnp.concatenate(
        [ratio[:, r * LANES : (r + 1) * LANES] for r in range(site_rows)], axis=0
    )
    eta = volt - 0.5 * jnp.log(ratio)
    current = live * rate_ref[...] * (jnp.exp(0.6 * eta) - jnp.exp(-0.4 * eta))

    spread_current = jnp.concatenate(
        [
            jnp.where(sub == spread(site_slot, r), spread(current, r), 0.0)
            for r in range(site_rows)
        ],
        axis=1,
    )
    high = spread_current.astype(jnp.bfloat16).astype(jnp.float32)
    rest = spread_current - high
    middle = rest.astype(jnp.bfloat16).astype(jnp.float32)
    low = rest - middle
    parts = jnp.concatenate([high, middle, low, jnp.zeros_like(low)], axis=0).astype(jnp.bfloat16)
    sums = lax.dot_general(
        parts, onehot[...], (((1,), (1,)), ((), ())), preferred_element_type=jnp.float32
    )
    sums = sums[0:8] + sums[8:16] + sums[16:24]
    for k in range(SLOTS):
        bucket[k] = sums[k : k + 1]
    send_pores(3)

    def look_up(tab, key, lane):
        found = [zero, zero]
        for k in range(SLOTS):
            for seg in range(segs):
                hit = key == k * segs + seg
                for c in range(2):
                    row = tab[k, c : c + 1, seg * LANES : (seg + 1) * LANES]
                    got = jnp.take_along_axis(jnp.broadcast_to(row, (8, LANES)), lane, axis=1)
                    found[c] = jnp.where(hit, got, found[c])
        return found

    def diffuse(tab):
        near = ([], [])
        for j in range(segs):
            cut = slice(j * LANES, (j + 1) * LANES)
            a, b = look_up(tab, near_key[:, cut], near_lane[:, cut])
            near[0].append(a)
            near[1].append(b)
        sum_a = jnp.sum(masked * jnp.concatenate(near[0], axis=1), axis=0, keepdims=True)
        sum_b = jnp.sum(masked * jnp.concatenate(near[1], axis=1), axis=0, keepdims=True)
        mag_a = jnp.abs(tab[0, 0:1])
        mag_b = jnp.abs(tab[0, 1:2])
        size = mag_a + mag_b + 1.0
        diff_a = DK_A / (1.0 + DK_A / DIFF_M * mag_b / size)
        diff_b = DK_B / (1.0 + DK_B / DIFF_M * mag_a / size)
        return (
            diff_a * sum_a + exch * BATH_A,
            diff_b * sum_b + exch * BATH_B,
            diff_a * wsum + exch,
            diff_b * wsum + exch,
        )

    await_pores(0)
    drawn = None
    for sweep in range(SWEEPS_G):
        top_a, top_b, bottom_a, bottom_b = diffuse(tabs[sweep])
        if sweep == 0:
            await_pores(3)
            drawn = bucket[0]
            for k in range(6):
                drawn = drawn + arrived[1 + k]
            drawn = CURRENT_SCALE * drawn
        new_a = (top_a - drawn) / bottom_a
        new_b = (top_b + drawn) / bottom_b
        tabs[sweep + 1][0, 0:1] = new_a
        tabs[sweep + 1][0, 1:2] = new_b
        send_pores(sweep + 1)
        if sweep == SWEEPS_G - 1:
            press_out[0:1, :] = new_a
            press_out[1:2, :] = new_b
        await_pores(sweep + 1)

    found = look_up(tabs[SWEEPS_G], site_key, site_lane)
    for c in range(2):
        values = found[c] * live
        for r in range(site_rows):
            tile_out[c : c + 1, r * LANES : (r + 1) * LANES] = values[r : r + 1]

    for e in range(5):
        for side in (0, 1):

            @pl.when(there[side])
            def _():
                x_copy(e, side).wait_send()

            for chunk in range(CHUNKS):

                @pl.when(there[2 + side])
                def _():
                    y_copy(e, side, chunk).wait_send()

                @pl.when(there[4 + side])
                def _():
                    z_copy(e, side, chunk).wait_send()

    for e in range(4):
        for k in range(6):

            @pl.when(there[k])
            def _():
                p_copy(e, k).wait_send()

    for chunk in range(CHUNKS):
        rows = pl.ds(chunk * nc, nc)
        pltpu.make_async_copy(fin.at[rows], phi_out.at[rows], out_sem.at[chunk]).wait()


def body(
    labels,
    conduct_scale,
    phase_sigma,
    source,
    potential_in,
    site_voxel,
    site_owner,
    site_pore,
    site_live,
    site_rate,
    tile_press_in,
    throat_nbr,
    throat_count,
    throat_weight,
    pore_exchange,
    pore_press_in,
):
    sizes = (lax.axis_size("gx"), lax.axis_size("gy"), lax.axis_size("gz"))
    nx, ny, nz = source.shape
    pores = pore_exchange.shape[0]
    sites = site_voxel.shape[0]
    f32 = jnp.float32

    def brick(extra=0):
        return pltpu.VMEM((nx + extra, ny, nz), f32)

    dma = pltpu.SemaphoreType.DMA
    any_spec = pl.BlockSpec(memory_space=pl.ANY)
    vmem = pl.BlockSpec(memory_space=pltpu.VMEM)
    by_row = (sites // LANES, LANES)
    return pl.pallas_call(
        functools.partial(kernel, sizes),
        out_shape=(
            jax.ShapeDtypeStruct((nx, ny, nz), f32),
            jax.ShapeDtypeStruct((2, pores), f32),
            jax.ShapeDtypeStruct((2, sites), f32),
        ),
        in_specs=[pl.BlockSpec(memory_space=pltpu.SMEM)] + [any_spec] * 4 + [vmem] * 11,
        out_specs=(any_spec, vmem, vmem),
        scratch_shapes=[
            pltpu.VMEM((nx, ny, nz), jnp.int32),
            brick(),
            brick(),
            brick(2),
            brick(2),
            brick(2),
            brick(2),
            brick(2),
            brick(),
            brick(1),
            brick(),
            brick(),
            brick(),
            pltpu.VMEM((5, nx, 1, nz), f32),
            pltpu.VMEM((5, nx, 1, nz), f32),
            pltpu.VMEM((5, nx, 1, nz), f32),
            pltpu.VMEM((5, nx, 1, nz), f32),
            pltpu.VMEM((5, nx, ny, LANES), f32),
            pltpu.VMEM((5, nx, ny, LANES), f32),
            pltpu.VMEM((pores, sites), jnp.bfloat16),
            pltpu.VMEM((SLOTS, 2, pores), f32),
            pltpu.VMEM((SLOTS, 2, pores), f32),
            pltpu.VMEM((SLOTS, 2, pores), f32),
            pltpu.VMEM((SLOTS, 1, pores), f32),
            pltpu.VMEM((SLOTS, 1, pores), f32),
            dma((4, CHUNKS)),
            dma((CHUNKS,)),
            dma((5, 2)),
            dma((5, 2)),
            dma((5, 2, CHUNKS)),
            dma((5, 2, CHUNKS)),
            dma((5, 2, CHUNKS)),
            dma((5, 2, CHUNKS)),
            dma((4, 6)),
            dma((4, 6)),
        ],
        compiler_params=pltpu.CompilerParams(
            collective_id=0, has_side_effects=True, vmem_limit_bytes=58 * 1024 * 1024
        ),
    )(
        phase_sigma,
        labels,
        conduct_scale,
        source,
        potential_in,
        site_voxel.reshape(by_row),
        site_owner.reshape(by_row),
        site_pore.reshape(by_row),
        site_live.reshape(by_row),
        site_rate.reshape(by_row),
        tile_press_in,
        throat_nbr,
        throat_count.reshape(1, pores),
        throat_weight,
        pore_exchange.reshape(1, pores),
        pore_press_in,
    )


def solution(mesh):
    return jax.shard_map(
        body,
        mesh=mesh,
        in_specs=(
            P("gx", "gy", "gz"),
            P("gx", "gy", "gz"),
            P(),
            P("gx", "gy", "gz"),
            P("gx", "gy", "gz"),
            P(("gx", "gy", "gz")),
            P(("gx", "gy", "gz")),
            P(("gx", "gy", "gz")),
            P(("gx", "gy", "gz")),
            P(("gx", "gy", "gz")),
            P(None, ("gx", "gy", "gz")),
            P(None, ("gx", "gy", "gz")),
            P(("gx", "gy", "gz")),
            P(None, ("gx", "gy", "gz")),
            P(("gx", "gy", "gz")),
            P(None, ("gx", "gy", "gz")),
        ),
        out_specs=(P("gx", "gy", "gz"), P(None, ("gx", "gy", "gz")), P(None, ("gx", "gy", "gz"))),
        check_vma=False,
    )
```

time: 550 us -> 63.7 us (0.12)
  blocking collectives: 214 us -> 0 us
  starting transfers between devices: 114 us -> 0 us
  other arithmetic: 100 us -> 0 us
  local copies, waits for them, and re-layouts: 90.3 us -> 4.39 us
  Pallas kernels: 0 us -> 58.4 us
  waiting for transfers between devices: 27.4 us -> 0 us
    all_gather x2 -> x0, blocking collectives: 214 us -> none  [body(): whole = lax.all_gather(press, ('gx', 'gy', 'gz'), axis=1, tiled=True)]
    ppermute x42 -> x0, starting transfers between devices: 114 us -> none  [the longest x21 86.8 us: extended(): before = lax.ppermute(last, axis, up)]
    select_n x4 -> x0, other arithmetic: 73.6 us -> none  [relax(): return jnp.where(centre > 0.0, numer / denom, 0.0)]
    pallas_call x0 -> x1, Pallas kernels: none -> 58.4 us  [body(): pl.pallas_call(functools.partial(kernel, sizes), out_shape=(jax.ShapeDtyp...]
    gather x6 -> x0, local copies, waits for them, and re-layouts: 41.5 us -> none  [the longest x4 29.6 us: body(): near = whole[:, throat_nbr]]
    ppermute x42 -> x0, waiting for transfers between devices: 27.4 us -> none  [the longest x21 18.6 us: extended(): after = lax.ppermute(leading, axis, down)]
    slice x22 -> x0, local copies, waits for them, and re-layouts: 19 us -> none  [the longest x13 9.42 us: extended(): last = lax.slice_in_dim(array, length - width, length, axis=dim)]
    ppermute x10 -> x0, local copies, waits for them, and re-layouts: 18.3 us -> none  [the longest x5 9.15 us: extended(): after = lax.ppermute(leading, axis, down)]
  transfers between devices with their start and end apart: 42 -> 0, of which waited for: 16 -> 0; matrix products, arithmetic and copies ran while one was open for 8% -> 0% of each run, Pallas kernels for 0% -> 0%
where the time goes in v1:
time: 63.7 us; the launch traced here: 63.5 us
  Pallas kernels  58.4 us (92%)
  local copies, waits for them, and re-layouts  4.39 us (7%)
  between operations  0.66 us (1%)
    pallas_call x1, Pallas kernels, body(): pl.pallas_call(functools.partial(kernel, sizes), out_shape=(jax.ShapeDtyp...  58.4 us
    unnamed x7, local copies, waits for them, and re-layouts  4.39 us

profile of v1, /device:TPU:0, one launch (start us, length us, event | category | flops | bytes accessed | tf_op | source)
XLA Modules:
  0.0 63.5 jit_solution(5345867604882614045)
XLA Ops:
  0.6 58.4 %shard_map.175 = (f32[32,32,512]{2,1,0:T(8,128)}, f32[2,512]{1,0:T(2,128)}, f32[2,1024]{1,0:T(2,128)}) custom-call(f32[3]{0:T(128)} %table_ref.1, s32[32,32,512]{2,1,0:T(8,128)} %lab_hbm.1, f32[32,32,512]{2,1,0:T(8,128)} %cs_hbm.1, f32[32,32,512]{2,1,0:T(8,128)} %src_hbm.1, f32[32,32,512]{2,1,0:T(8,128)} %phi_hbm.1, s32[8,128]{1,0:T(8,128)} %bitcast.7, ...), custom_call_target="tpu_custom_call" | custom-call | tf_op jit(solution)/shard_map/pallas_call | solution.py:588
  59.0 0.0 copy-start.1
  59.1 0.0 copy-start
  59.1 3.2 %copy.22 = f32[32,32,512]{2,1,0:T(8,128)} copy(f32[32,32,512]{2,1,0:T(8,128)} %get-tuple-element.6) | data formatting | bytes 4194304
  62.3 0.0 copy-done.1
  62.3 0.6 copy.23
  62.9 0.0 copy-done
  62.9 0.6 copy.24
Async XLA Ops:
  59.0 3.2 %copy-start.1 = (f32[2,512]{1,0:T(2,128)S(1)}, f32[2,512]{1,0:T(2,128)}, u32[]{:S(2)}) copy-start(f32[2,512]{1,0:T(2,128)} %get-tuple-element.7) | copy-start | bytes 12292
  59.1 3.8 %copy-start = (f32[2,1024]{1,0:T(2,128)S(1)}, f32[2,1024]{1,0:T(2,128)}, u32[]{:S(2)}) copy-start(f32[2,1024]{1,0:T(2,128)} %get-tuple-element.8) | copy-start | bytes 24580

commit v2 on v1

--- a/solution.py
+++ b/solution.py
@@ -24,22 +24,17 @@
 MESH = pl.DeviceIdType.MESH
 
 
-def up_z(v, after):
-    ext = jnp.concatenate([v, after], axis=1)
-    return pltpu.roll(ext, ext.shape[1] - 1, 1)[:, : v.shape[1]]
-
-
-def down_z(v, before):
-    ext = jnp.concatenate([before, v], axis=1)
-    return pltpu.roll(ext, 1, 1)[:, before.shape[1] :]
-
-
-def up_y(v, row, is_last):
-    return jnp.where(is_last, row, pltpu.roll(v, v.shape[0] - 1, 0))
-
-
-def down_y(v, row, is_first):
-    return jnp.where(is_first, row, pltpu.roll(v, 1, 0))
+TOP = 8
+
+
+def up_z(blocks, after, is_last):
+    turned = [pltpu.roll(v, LANES - 1, 1) for v in [*blocks, after]]
+    return [jnp.where(is_last, b, a) for a, b in zip(turned[:-1], turned[1:])]
+
+
+def down_z(blocks, before, is_first):
+    turned = [pltpu.roll(v, 1, 1) for v in [before, *blocks]]
+    return [jnp.where(is_first, a, b) for a, b in zip(turned[:-1], turned[1:])]
 
 
 def kernel(
@@ -75,11 +70,8 @@
     gxf,
     gyf,
     gzf,
+    glow,
     inv,
-    ylo,
-    yhi,
-    ysend_lo,
-    ysend_hi,
     zlo,
     zhi,
     onehot,
@@ -100,8 +92,10 @@
     pr_sem,
 ):
     size_x, size_y, size_z = sizes
-    nx, ny, nz = src.shape
+    nx, zts, ny, _ = src.shape
+    nz = zts * LANES
     nc = nx // CHUNKS
+    inside = pl.ds(TOP, ny)
     pores = press_ref.shape[1]
     segs = pores // LANES
     ix, iy, iz = (lax.axis_index("gx"), lax.axis_index("gy"), lax.axis_index("gz"))
@@ -113,16 +107,30 @@
         there += [at > 0, at < size - 1]
         where_to += [{name: at - 1}, {name: at + 1}]
 
-    def load(which, chunk):
+    def load(which, chunk, zt):
         rows = pl.ds(chunk * nc, nc)
         far, near = ((lab_hbm, lab), (cs_hbm, cs), (phi_hbm, phi0), (src_hbm, src))[which]
-        inner = pl.ds(1 + chunk * nc, nc) if which == 2 else rows
-        return pltpu.make_async_copy(far.at[rows], near.at[inner], load_sem.at[which, chunk])
+        if which == 2:
+            near = near.at[pl.ds(1 + chunk * nc, nc), zt, inside]
+        else:
+            near = near.at[rows, zt]
+        return pltpu.make_async_copy(
+            far.at[rows, :, pl.ds(zt * LANES, LANES)], near, load_sem.at[which, chunk, zt]
+        )
+
+    def unload(chunk, zt):
+        rows = pl.ds(chunk * nc, nc)
+        return pltpu.make_async_copy(
+            fin.at[rows, zt],
+            phi_out.at[rows, :, pl.ds(zt * LANES, LANES)],
+            out_sem.at[chunk, zt],
+        )
 
     for part in ((0, 1), (2,), (3,)):
         for chunk in ORDER:
             for which in part:
-                load(which, chunk).start()
+                for zt in range(zts):
+                    load(which, chunk, zt).start()
 
     barrier = pltpu.get_barrier_semaphore()
     total = jnp.int32(0)
@@ -138,8 +146,8 @@
     def x_copy(e, side):
         field = fields[e]
         return pltpu.make_async_remote_copy(
-            src_ref=field.at[1 if side == 0 else nx],
-            dst_ref=field.at[nx + 1 if side == 0 else 0],
+            src_ref=field.at[1 if side == 0 else nx, :, inside],
+            dst_ref=field.at[nx + 1 if side == 0 else 0, :, inside],
             send_sem=xs_sem.at[e, side],
             recv_sem=xr_sem.at[e, 1 - side],
             device_id=where_to[side],
@@ -147,10 +155,11 @@
         )
 
     def y_copy(e, side, chunk):
-        rows = pl.ds(chunk * nc, nc)
+        rows = pl.ds(1 + chunk * nc, nc)
+        first, final = (TOP, TOP + ny - 1)
         return pltpu.make_async_remote_copy(
-            src_ref=(ysend_lo if side == 0 else ysend_hi).at[e, rows],
-            dst_ref=(yhi if side == 0 else ylo).at[e, rows],
+            src_ref=fields[e].at[rows, :, pl.ds(first if side == 0 else final, 1)],
+            dst_ref=fields[e].at[rows, :, pl.ds(final + 1 if side == 0 else first - 1, 1)],
             send_sem=ys_sem.at[e, side, chunk],
             recv_sem=yr_sem.at[e, 1 - side, chunk],
             device_id=where_to[2 + side],
@@ -160,7 +169,7 @@
     def z_copy(e, side, chunk):
         return pltpu.make_async_remote_copy(
             src_ref=fields[e].at[
-                pl.ds(1 + chunk * nc, nc), :, pl.ds(0 if side == 0 else nz - LANES, LANES)
+                pl.ds(1 + chunk * nc, nc), 0 if side == 0 else zts - 1, inside
             ],
             dst_ref=(zhi if side == 0 else zlo).at[e, pl.ds(chunk * nc, nc)],
             send_sem=zs_sem.at[e, side, chunk],
@@ -243,16 +252,22 @@
             def _():
                 p_copy(e, k ^ 1).wait_recv()
 
-    for side, (xat, ybuf, zbuf) in enumerate(((0, ylo, zlo), (nx + 1, yhi, zhi))):
+    for side, (xat, yat, zbuf) in enumerate(((0, TOP - 1, zlo), (nx + 1, TOP + ny, zhi))):
 
         @pl.when(jnp.logical_not(there[side]))
         def _():
             for field in fields:
-                field[xat] = jnp.zeros((ny, nz), jnp.float32)
+                field[xat, :, inside] = jnp.zeros((zts, ny, LANES), jnp.float32)
 
         @pl.when(jnp.logical_not(there[2 + side]))
         def _():
-            ybuf[...] = jnp.zeros(ybuf.shape, jnp.float32)
+            def clear_row(i, carry):
+                for field in fields:
+                    for zt in range(zts):
+                        field[i + 1, zt, yat : yat + 1] = jnp.zeros((1, LANES), jnp.float32)
+                return carry
+
+            lax.fori_loop(0, nx, clear_row, 0)
 
         @pl.when(jnp.logical_not(there[4 + side]))
         def _():
@@ -279,28 +294,22 @@
 
     s0, s1, s2 = (table_ref[0], table_ref[1], table_ref[2])
     for chunk in ORDER:
-        load(0, chunk).wait()
-        load(1, chunk).wait()
+        for zt in range(zts):
+            load(0, chunk, zt).wait()
+            load(1, chunk, zt).wait()
 
         def conductivity(i, carry):
             kind = lab[i]
-            value = cs[i] * jnp.where(kind == 0, s0, jnp.where(kind == 1, s1, s2))
-            sig[i + 1] = value
-            ysend_lo[0, i] = value[0:1]
-            ysend_hi[0, i] = value[ny - 1 : ny]
+            sig[i + 1, :, inside] = cs[i] * jnp.where(
+                kind == 0, s0, jnp.where(kind == 1, s1, s2)
+            )
             return carry
 
         lax.fori_loop(chunk * nc, (chunk + 1) * nc, conductivity, 0)
         send_faces(0, chunk)
     for chunk in ORDER:
-        load(2, chunk).wait()
-
-        def pack(i, carry):
-            ysend_lo[1, i] = phi0[i + 1, 0:1]
-            ysend_hi[1, i] = phi0[i + 1, ny - 1 : ny]
-            return carry
-
-        lax.fori_loop(chunk * nc, (chunk + 1) * nc, pack, 0)
+        for zt in range(zts):
+            load(2, chunk, zt).wait()
         send_faces(1, chunk)
 
     own = (ix * size_y + iy) * size_z + iz
@@ -331,9 +340,11 @@
         hit = jnp.where(pore_no == site_pore[r : r + 1], 1.0, 0.0)
         onehot[:, r * LANES : (r + 1) * LANES] = hit.astype(jnp.bfloat16)
 
-    y_no = lax.broadcasted_iota(jnp.int32, (ny, nz), 0)
-    y_first = y_no == 0
-    y_last = y_no == ny - 1
+    z_no = lax.broadcasted_iota(jnp.int32, (ny, LANES), 1)
+    z_first = z_no == 0
+    z_last = z_no == LANES - 1
+    low_y = pl.ds(TOP - 1, ny)
+    high_y = pl.ds(TOP + 1, ny)
 
     for sweep in range(SWEEPS_E):
         old = fields[1 + sweep]
@@ -342,104 +353,96 @@
         for chunk in ORDER:
             if sweep == 0:
                 await_faces(0, chunk)
-                load(3, chunk).wait()
+                for zt in range(zts):
+                    load(3, chunk, zt).wait()
             await_faces(e, chunk)
 
             def relax(i, carry):
-                phi = old[i + 1]
+                tiles = range(zts)
+                phi = [old[i + 1, zt, inside] for zt in tiles]
                 if sweep == 0:
-                    s = sig[i + 1]
-                    g_below = 0.5 * (sig[i] + s)
-                    g_above = 0.5 * (s + sig[i + 2])
-                    gy = 0.5 * (s + up_y(s, yhi[0, i], y_last))
-                    gz = 0.5 * (s + up_z(s, zhi[0, i]))
-                    y_low = 0.5 * (ylo[0, i] + s[0:1])
-                    gxf[i] = g_below
-                    gxf[i + 1] = g_above
-                    gyf[i] = gy
-                    gzf[i] = gz
-                    z_low = 0.5 * (zlo[0, i] + pltpu.roll(s[:, :LANES], LANES - 1, 1))
-                    ylo[0, i] = y_low
+                    s = [sig[i + 1, zt, inside] for zt in tiles]
+                    after = up_z(s, zhi[0, i], z_last)
+                    gz = [0.5 * (s[zt] + after[zt]) for zt in tiles]
+                    z_low = 0.5 * (zlo[0, i] + pltpu.roll(s[0], LANES - 1, 1))
                     zlo[0, i] = z_low
-                    denom = (
-                        REACT
-                        + g_below
-                        + g_above
-                        + gy
-                        + down_y(gy, y_low, y_first)
-                        + gz
-                        + down_z(gz, z_low)
+                    gz_below = down_z(gz, z_low, z_first)
+                    g = []
+                    for zt in tiles:
+                        near = [
+                            0.5 * (s[zt] + sig[i, zt, inside]),
+                            0.5 * (s[zt] + sig[i + 2, zt, inside]),
+                            0.5 * (s[zt] + sig[i + 1, zt, low_y]),
+                            0.5 * (s[zt] + sig[i + 1, zt, high_y]),
+                        ]
+                        denom = REACT + gz[zt] + gz_below[zt]
+                        for face in near:
+                            denom = denom + face
+                        scale = jnp.where(s[zt] > 0.0, 1.0 / denom, 0.0)
+                        inv[i, zt] = scale
+                        gxf[i, zt] = near[0]
+                        gxf[i + 1, zt] = near[1]
+                        glow[i, zt] = near[2]
+                        gyf[i, zt] = near[3]
+                        gzf[i, zt] = gz[zt]
+                        g.append((*near, scale))
+                else:
+                    gz = [gzf[i, zt] for zt in tiles]
+                    z_low = zlo[0, i]
+                    g = [
+                        (gxf[i, zt], gxf[i + 1, zt], glow[i, zt], gyf[i, zt], inv[i, zt])
+                        for zt in tiles
+                    ]
+                after = up_z(phi, zhi[e, i], z_last)
+                below = down_z([gz[zt] * phi[zt] for zt in tiles], z_low * zlo[e, i], z_first)
+                for zt in tiles:
+                    numer = (
+                        src[i, zt]
+                        + g[zt][0] * old[i, zt, inside]
+                        + g[zt][1] * old[i + 2, zt, inside]
+                        + g[zt][2] * old[i + 1, zt, low_y]
+                        + g[zt][3] * old[i + 1, zt, high_y]
+                        + gz[zt] * after[zt]
+                        + below[zt]
                     )
-                    scale = jnp.where(s > 0.0, 1.0 / denom, 0.0)
-                    inv[i] = scale
-                else:
-                    g_below = gxf[i]
-                    g_above = gxf[i + 1]
-                    gy = gyf[i]
-                    gz = gzf[i]
-                    y_low = ylo[0, i]
-                    z_low = zlo[0, i]
-                    scale = inv[i]
-                numer = (
-                    src[i]
-                    + g_below * old[i]
-                    + g_above * old[i + 2]
-                    + gy * up_y(phi, yhi[e, i], y_last)
-                    + down_y(gy * phi, y_low * ylo[e, i], y_first)
-                    + gz * up_z(phi, zhi[e, i])
-                    + down_z(gz * phi, z_low * zlo[e, i])
-                )
-                value = numer * scale
-                if last:
-                    fin[i] = value
-                else:
-                    fields[e + 1][i + 1] = value
-                    ysend_lo[e + 1, i] = value[0:1]
-                    ysend_hi[e + 1, i] = value[ny - 1 : ny]
+                    value = numer * g[zt][4]
+                    if last:
+                        fin[i, zt] = value
+                    else:
+                        fields[e + 1][i + 1, zt, inside] = value
                 return carry
 
             lax.fori_loop(chunk * nc, (chunk + 1) * nc, relax, 0)
             if last:
-                rows = pl.ds(chunk * nc, nc)
-                pltpu.make_async_copy(fin.at[rows], phi_out.at[rows], out_sem.at[chunk]).start()
+                for zt in range(zts):
+                    unload(chunk, zt).start()
             else:
                 send_faces(e + 1, chunk)
 
-    voxel = voxel_ref[...]
     y_bits, z_bits = (ny.bit_length() - 1, nz.bit_length() - 1)
-    vz = voxel & (nz - 1)
-    vy = (voxel >> z_bits) & (ny - 1)
-    vx = voxel >> (z_bits + y_bits)
-    y_tiles, z_tiles = (ny // 8, nz // LANES)
-    tile_no = (vx * y_tiles + (vy >> 3)) * z_tiles + (vz >> lane_bits)
     sub = lax.broadcasted_iota(jnp.int32, (8, LANES), 0)
+    lane_no = lax.broadcasted_iota(jnp.int32, (1, LANES), 1)
 
     def spread(a, r):
         return jnp.broadcast_to(a[r : r + 1], (8, LANES))
 
-    tile_rows = [spread(tile_no, r) for r in range(site_rows)]
-    lane_rows = [spread(vz & (LANES - 1), r) for r in range(site_rows)]
-
-    def pick(i, accs):
-        accs = list(accs)
-        for ty in range(y_tiles):
-            for tz in range(z_tiles):
-                block = fin[i, ty * 8 : ty * 8 + 8, tz * LANES : (tz + 1) * LANES]
-                here = (i * y_tiles + ty) * z_tiles + tz
-                for r in range(site_rows):
-                    got = jnp.take_along_axis(block, lane_rows[r], axis=1)
-                    accs[r] = jnp.where(tile_rows[r] == here, got, accs[r])
-        return tuple(accs)
+    def pick(j, volts):
+        here = lane_no == j
+        picked = []
+        for r in range(site_rows):
+            v = voxel_ref[r, j]
+            row = fin[
+                v >> (z_bits + y_bits),
+                (v >> lane_bits) & (zts - 1),
+                pl.ds((v >> z_bits) & (ny - 1), 1),
+            ]
+            row = pltpu.roll(row, (j - v) & (LANES - 1), 1)
+            picked.append(jnp.where(here, row, volts[r]))
+        return tuple(picked)
 
     zero = jnp.zeros((8, LANES), jnp.float32)
-    accs = lax.fori_loop(0, nx, pick, (zero,) * site_rows)
-    volt = jnp.concatenate(
-        [
-            jnp.sum(jnp.where(sub == spread(vy & 7, r), accs[r], 0.0), axis=0, keepdims=True)
-            for r in range(site_rows)
-        ],
-        axis=0,
-    )
+    volts = lax.fori_loop(0, LANES, pick, (zero[0:1],) * site_rows, unroll=4)
+    volt = jnp.concatenate(volts, axis=0)
     ratio = tpress_ref[1:2, :] / tpress_ref[0:1, :]
     ratio = jnp.concatenate(
         [ratio[:, r * LANES : (r + 1) * LANES] for r in range(site_rows)], axis=0
@@ -550,8 +553,8 @@
                 p_copy(e, k).wait_send()
 
     for chunk in range(CHUNKS):
-        rows = pl.ds(chunk * nc, nc)
-        pltpu.make_async_copy(fin.at[rows], phi_out.at[rows], out_sem.at[chunk]).wait()
+        for zt in range(zts):
+            unload(chunk, zt).wait()
 
 
 def body(
@@ -578,8 +581,13 @@
     sites = site_voxel.shape[0]
     f32 = jnp.float32
 
-    def brick(extra=0):
-        return pltpu.VMEM((nx + extra, ny, nz), f32)
+    zts = nz // LANES
+
+    def brick(extra=0, kind=f32):
+        return pltpu.VMEM((nx + extra, zts, ny, LANES), kind)
+
+    def field():
+        return pltpu.VMEM((nx + 2, zts, ny + 2 * TOP, LANES), f32)
 
     dma = pltpu.SemaphoreType.DMA
     any_spec = pl.BlockSpec(memory_space=pl.ANY)
@@ -592,26 +600,25 @@
             jax.ShapeDtypeStruct((2, pores), f32),
             jax.ShapeDtypeStruct((2, sites), f32),
         ),
-        in_specs=[pl.BlockSpec(memory_space=pltpu.SMEM)] + [any_spec] * 4 + [vmem] * 11,
+        in_specs=[pl.BlockSpec(memory_space=pltpu.SMEM)] + [any_spec] * 4
+        + [pl.BlockSpec(memory_space=pltpu.SMEM)]
+        + [vmem] * 10,
         out_specs=(any_spec, vmem, vmem),
         scratch_shapes=[
-            pltpu.VMEM((nx, ny, nz), jnp.int32),
+            brick(0, jnp.int32),
             brick(),
             brick(),
-            brick(2),
-            brick(2),
-            brick(2),
-            brick(2),
-            brick(2),
+            field(),
+            field(),
+            field(),
+            field(),
+            field(),
             brick(),
             brick(1),
             brick(),
             brick(),
             brick(),
-            pltpu.VMEM((5, nx, 1, nz), f32),
-            pltpu.VMEM((5, nx, 1, nz), f32),
-            pltpu.VMEM((5, nx, 1, nz), f32),
-            pltpu.VMEM((5, nx, 1, nz), f32),
+            brick(),
             pltpu.VMEM((5, nx, ny, LANES), f32),
             pltpu.VMEM((5, nx, ny, LANES), f32),
             pltpu.VMEM((pores, sites), jnp.bfloat16),
@@ -620,8 +627,8 @@
             pltpu.VMEM((SLOTS, 2, pores), f32),
             pltpu.VMEM((SLOTS, 1, pores), f32),
             pltpu.VMEM((SLOTS, 1, pores), f32),
-            dma((4, CHUNKS)),
-            dma((CHUNKS,)),
+            dma((4, CHUNKS, zts)),
+            dma((CHUNKS, zts)),
             dma((5, 2)),
             dma((5, 2)),
             dma((5, 2, CHUNKS)),

time: 63.7 us -> 56.8 us (0.89)
  Pallas kernels: 58.4 us -> 51.5 us
    pallas_call x1, Pallas kernels: 58.4 us -> 51.5 us  [body(): pl.pallas_call(functools.partial(kernel, sizes), out_shape=(jax.ShapeDtyp...]
where the time goes in v2:
time: 56.8 us; the launch traced here: 56.6 us
  Pallas kernels  51.5 us (91%)
  local copies, waits for them, and re-layouts  4.39 us (8%)
  between operations  0.66 us (1%)
    pallas_call x1, Pallas kernels, body(): pl.pallas_call(functools.partial(kernel, sizes), out_shape=(jax.ShapeDtyp...  51.5 us
    unnamed x7, local copies, waits for them, and re-layouts  4.39 us

profile of v2, /device:TPU:0, one launch (start us, length us, event | category | flops | bytes accessed | tf_op | source)
XLA Modules:
  0.0 56.6 jit_solution(16403239290379663492)
XLA Ops:
  0.6 51.5 %shard_map.175 = (f32[32,32,512]{2,1,0:T(8,128)}, f32[2,512]{1,0:T(2,128)}, f32[2,1024]{1,0:T(2,128)}) custom-call(f32[3]{0:T(128)} %table_ref.1, s32[32,32,512]{2,1,0:T(8,128)} %lab_hbm.1, f32[32,32,512]{2,1,0:T(8,128)} %cs_hbm.1, f32[32,32,512]{2,1,0:T(8,128)} %src_hbm.1, f32[32,32,512]{2,1,0:T(8,128)} %phi_hbm.1, s32[8,128]{1,0:T(8,128)} %bitcast.7, ...), custom_call_target="tpu_custom_call" | custom-call | tf_op jit(solution)/shard_map/pallas_call | solution.py:596
  52.1 0.0 copy-start.1
  52.2 0.0 copy-start
  52.2 3.2 %copy.22 = f32[32,32,512]{2,1,0:T(8,128)} copy(f32[32,32,512]{2,1,0:T(8,128)} %get-tuple-element.6) | data formatting | bytes 4194304
  55.4 0.0 copy-done.1
  55.4 0.6 %copy.23 = f32[2,512]{1,0:T(2,128)} copy(f32[2,512]{1,0:T(2,128)S(1)} %copy-done.1) | data formatting | bytes 8192
  56.0 0.0 copy-done
  56.0 0.6 %copy.24 = f32[2,1024]{1,0:T(2,128)} copy(f32[2,1024]{1,0:T(2,128)S(1)} %copy-done) | data formatting | bytes 16384
Async XLA Ops:
  52.1 3.2 %copy-start.1 = (f32[2,512]{1,0:T(2,128)S(1)}, f32[2,512]{1,0:T(2,128)}, u32[]{:S(2)}) copy-start(f32[2,512]{1,0:T(2,128)} %get-tuple-element.7) | copy-start | bytes 12292
  52.2 3.8 %copy-start = (f32[2,1024]{1,0:T(2,128)S(1)}, f32[2,1024]{1,0:T(2,128)}, u32[]{:S(2)}) copy-start(f32[2,1024]{1,0:T(2,128)} %get-tuple-element.8) | copy-start | bytes 24580
